TPU v7x, 32 devices: a whole 2x2x4 slice. The times are simulated.
32 devices in a mesh: space: 16 (over z, x, core), chan: 2 (over y).
Axes of the slice: x: 2, y: 2, z: 4, core: 2. Of those that a mesh axis runs over, the one named last changes fastest.
Arguments:
- features: bfloat16 [16384, 256], P('space', 'chan'), may hold values from -6 to 6
- weights: bfloat16 [27, 256, 256], P(None, 'chan'), may hold values from -0.125 to 0.125
- send_rows: int32 [16, 8, 768], P('space'), may hold values from 0 to 1024, as said below
- gather_map: int32 [27, 16384], P(None, 'space'), may hold values from 0 to 7168, as said below
Outputs:
- output: bfloat16 [16384, 256], P('space', 'chan')
Inputs may be any that keep to these rules, and one draw needn't show every extreme that they name: `send_rows`: an entry of 1024 marks an empty slot; the others are local row numbers of the sending block. Every direction of every block has some empty slots. `gather_map`: an entry of 7168 names the zero row; offset 13 (the centre) maps each voxel to its own local row.
All inputs are finite; a program needn't handle non-finite values.
Results may differ from a plain program's by a relative error of at most 0.001.
Values may be sent and summed in bfloat16 or wider, within the bound.
A program may use at most 64 MiB of HBM per device.

v0:
```python
import jax
import jax.numpy as jnp
from jax import lax
from jax.sharding import PartitionSpec as P

GRID_COLS = 8


directions = [(-1, -1), (-1, 0), (-1, 1), (0, -1), (0, 1), (1, -1), (1, 0), (1, 1)]


def shifted(value, axis, steps):
    count = lax.axis_size(axis)
    first, last = (max(0, -steps), min(count, count - steps))
    return lax.ppermute(value, axis, [(source, source + steps) for source in range(first, last)])


def inside_grid(grid_row, grid_col, grid_rows):
    return (grid_row >= 0) & (grid_row < grid_rows) & (grid_col >= 0) & (grid_col < GRID_COLS)


def local(features, weights, send_rows, gather_map):
    group_width = features.shape[1]
    spaces = lax.axis_size("space")
    grid_rows = spaces // GRID_COLS
    myself = lax.axis_index("space")
    my_row = myself // GRID_COLS
    my_col = myself % GRID_COLS
    padded = jnp.concatenate([features, jnp.zeros((1, group_width), jnp.bfloat16)], axis=0)
    outgoing = padded[send_rows[0]]
    slots = outgoing.shape[1]
    pieces = []
    for number, (step_x, step_y) in enumerate(directions):
        got = shifted(outgoing[number], "space", step_x * GRID_COLS + step_y)
        usable = inside_grid(my_row - step_x, my_col - step_y, grid_rows)
        pieces.append(jnp.where(usable, got, jnp.zeros_like(got)))
    received = jnp.stack(pieces, axis=0)
    table = jnp.concatenate(
        [
            features,
            received.reshape(8 * slots, group_width),
            jnp.zeros((1, group_width), jnp.bfloat16),
        ],
        axis=0,
    )
    picked = table[gather_map]
    partial_value = jnp.einsum("kvc,kco->vo", picked, weights, preferred_element_type=jnp.float32)
    summed = lax.psum_scatter(partial_value, "chan", scatter_dimension=1, tiled=True)
    return summed.astype(jnp.bfloat16)


def solution(mesh):
    in_specs = (P("space", "chan"), P(None, "chan", None), P("space", None, None), P(None, "space"))
    out_specs = P("space", "chan")
    return jax.shard_map(local, mesh=mesh, in_specs=in_specs, out_specs=out_specs, check_vma=False)
```

profile of v0, /device:TPU:2, one launch (start us, length us, event | category | flops | bytes accessed | tf_op | source)
XLA Modules:
  0.0 227.4 jit_solution(13618297452975674162)
XLA Ops:
  6.5 0.9 compare_select_fusion.1
  7.4 1.0 concatenate.6
  8.4 22.3 %gather_fusion = bf16[6144,128]{1,0:T(8,128)(2,1)} fusion(bf16[1025,128]{1,0:T(8,128)(2,1)S(1)} %concatenate.6, s32[6144]{0:T(1024)S(1)} %broadcast_clamp_fusion.1), kind=kCustom, calls=%fused_computation | custom fusion | bytes 3170304 | tf_op jit(solution)/shard_map/gather | solution.py:30
  30.7 2.3 fusion
  32.9 4.6 %collective-permute-start.7 = (bf16[768,128]{1,0:T(8,128)(2,1)S(1)}, bf16[768,128]{1,0:T(8,128)(2,1)}, u32[]{:S(2)}, u32[]{:S(2)}) collective-permute-start(bf16[768,128]{1,0:T(8,128)(2,1)S(1)} %get-tuple-element.5), channel_id=1, source_target_pairs={{0,18},{2,20},{4,22},{6,24},{8,26},{10,28},{12,30},{1,19},{3,21},{... | collective-permute-start | bytes 589832 | tf_op jit(solution)/shard_map/ppermute | solution.py:15
  37.5 2.0 collective-permute-start.6
  39.5 2.0 collective-permute-start.5
  41.5 3.6 %collective-permute-start.4 = (bf16[768,128]{1,0:T(8,128)(2,1)S(1)}, bf16[768,128]{1,0:T(8,128)(2,1)}, u32[]{:S(2)}, u32[]{:S(2)}) collective-permute-start(bf16[768,128]{1,0:T(8,128)(2,1)S(1)} %get-tuple-element.8), channel_id=1, source_target_pairs={{0,2},{2,4},{4,6},{6,8},{8,10},{10,12},{12,14},{14,16},{16,18},{18... | collective-permute-start | bytes 589832 | tf_op jit(solution)/shard_map/ppermute | solution.py:15
  45.0 1.3 collective-permute-start
  46.5 16.6 %collective-permute-done = bf16[768,128]{1,0:T(8,128)(2,1)} collective-permute-done((bf16[768,128]{1,0:T(8,128)(2,1)}, bf16[768,128]{1,0:T(8,128)(2,1)}, u32[]{:S(2)}, u32[]{:S(2)}) %collective-permute-start) | collective-permute-done | bytes 196640 | tf_op jit(solution)/shard_map/ppermute | solution.py:15
  63.1 1.4 collective-permute-start.1
  64.5 1.0 bitcast_dynamic-update-slice_fusion.7
  65.5 7.9 %collective-permute-done.1 = bf16[768,128]{1,0:T(8,128)(2,1)S(1)} collective-permute-done((bf16[768,128]{1,0:T(8,128)(2,1)S(1)}, bf16[768,128]{1,0:T(8,128)(2,1)S(1)}, u32[]{:S(2)}, u32[]{:S(2)}) %collective-permute-start.1) | collective-permute-done | bytes 196640 | tf_op jit(solution)/shard_map/ppermute | solution.py:15
  73.4 1.3 collective-permute-start.2
  74.7 0.1 bitcast_dynamic-update-slice_fusion.6
  74.8 9.0 %collective-permute-done.2 = bf16[768,128]{1,0:T(8,128)(2,1)S(1)} collective-permute-done((bf16[768,128]{1,0:T(8,128)(2,1)S(1)}, bf16[768,128]{1,0:T(8,128)(2,1)S(1)}, u32[]{:S(2)}, u32[]{:S(2)}) %collective-permute-start.2) | collective-permute-done | bytes 196640 | tf_op jit(solution)/shard_map/ppermute | solution.py:15
  83.7 2.5 %collective-permute-start.3 = (bf16[768,128]{1,0:T(8,128)(2,1)S(1)}, bf16[768,128]{1,0:T(8,128)(2,1)S(1)}, u32[]{:S(2)}, u32[]{:S(2)}) collective-permute-start(bf16[768,128]{1,0:T(8,128)(2,1)S(1)} %get-tuple-element.9), channel_id=1, source_target_pairs={{2,0},{4,2},{6,4},{8,6},{10,8},{12,10},{14,12},{16,14},{18,16},{20... | collective-permute-start | bytes 589832 | tf_op jit(solution)/shard_map/ppermute | solution.py:15
  86.3 0.1 bitcast_dynamic-update-slice_fusion.5
  86.3 3.1 %collective-permute-done.3 = bf16[768,128]{1,0:T(8,128)(2,1)S(1)} collective-permute-done((bf16[768,128]{1,0:T(8,128)(2,1)S(1)}, bf16[768,128]{1,0:T(8,128)(2,1)S(1)}, u32[]{:S(2)}, u32[]{:S(2)}) %collective-permute-start.3) | collective-permute-done | bytes 196640 | tf_op jit(solution)/shard_map/ppermute | solution.py:15
  89.4 0.1 bitcast_dynamic-update-slice_fusion.4
  89.5 0.0 collective-permute-done.4
  89.5 1.0 bitcast_dynamic-update-slice_fusion.3
  90.5 0.0 collective-permute-done.5
  90.5 0.1 bitcast_dynamic-update-slice_fusion.2
  90.6 0.1 bitcast_dynamic-update-slice_fusion.1
  90.7 0.1 bitcast_dynamic-update-slice_fusion
  90.8 7.3 %maximum_maximum_fusion = bf16[7169,128]{1,0:T(8,128)(2,1)} fusion(bf16[6144,128]{1,0:T(8,128)(2,1)S(1)} %bitcast.28, bf16[1024,128]{1,0:T(8,128)(2,1)S(1)} %copy-done.1, bf16[7169]{0:T(1024)(128)(2,1)S(1)} %pad.3.clone), kind=kLoop, calls=%fused_computation.2 | loop fusion | flops 5505792 | bytes 3684610 | tf_op jit(solution)/shard_map/concatenate | solution.py:38
  98.1 94.8 %gather_fusion.1 = bf16[27648,128]{1,0:T(8,128)(2,1)} fusion(bf16[7169,128]{1,0:T(8,128)(2,1)} %maximum_maximum_fusion, s32[27648]{0:T(1024)S(1)} %broadcast_clamp_fusion), kind=kCustom, calls=%fused_computation.1 | custom fusion | bytes 14266368 | tf_op jit(solution)/shard_map/gather | solution.py:46
  192.9 5.3 %convolution_bitcast_fusion = f32[1024,256]{1,0:T(8,128)} fusion(bf16[27,1024,128]{2,1,0:T(8,128)(2,1)} %bitcast.27, bf16[27,128,256]{2,1,0:T(8,128)(2,1)S(1)} %copy-done), kind=kOutput, calls=%fused_computation.3 | convolution fusion | flops 1811939328 | bytes 9895936 | tf_op jit(solution)/shard_map/kvc,kco->vo/dot_general | solution.py:47
  198.2 0.0 reduce-scatter.2.cloned.1.call-update
  198.2 20.5 %reduce-scatter.2.cloned.1.call-done = f32[1024,128]{1,0:T(8,128)} async-done(((f32[1024,256]{1,0:T(8,128)}), f32[1024,128]{1,0:T(8,128)}) %reduce-scatter.2.cloned.1.call-update) | async-done | bytes 524304 | tf_op jit(solution)/shard_map/reduce_scatter | solution.py:48
  218.8 1.8 convert_element_type.3
  (15 shorter events, 0.1 us)
Async XLA Ops:
  6.5 186.4 %copy-start = (bf16[27,128,256]{2,1,0:T(8,128)(2,1)S(1)}, bf16[27,128,256]{2,1,0:T(8,128)(2,1)}, u32[]{:S(2)}) copy-start(bf16[27,128,256]{2,1,0:T(8,128)(2,1)} %param.5) | copy-start | bytes 5308420
  6.5 212.2 %reduce-scatter.2.cloned.1.call-start = ((), (), s32[]{:S(2)}) async-start(), calls=%async_computation.1 | async-start | bytes 1572864 | tf_op jit(solution)/shard_map/reduce_scatter | solution.py:48
  30.7 15.7 %copy-start.2 = (s32[27,1024]{1,0:T(8,128)S(1)}, s32[27,1024]{1,0:T(8,128)}, u32[]{:S(2)}) copy-start(s32[27,1024]{1,0:T(8,128)} %param.7) | copy-start | bytes 331780
  32.9 57.7 %collective-permute-start.7 = (bf16[768,128]{1,0:T(8,128)(2,1)S(1)}, bf16[768,128]{1,0:T(8,128)(2,1)}, u32[]{:S(2)}, u32[]{:S(2)}) collective-permute-start(bf16[768,128]{1,0:T(8,128)(2,1)S(1)} %get-tuple-element.5), channel_id=1, source_target_pairs={{0,18},{2,20},{4,22},{6,24},{8,26},{10,28},{12,30},{1,19},{3,21},{... | collective-permute-start | bytes 589832 | tf_op jit(solution)/shard_map/ppermute | solution.py:15
  37.5 53.0 %collective-permute-start.6 = (bf16[768,128]{1,0:T(8,128)(2,1)S(1)}, bf16[768,128]{1,0:T(8,128)(2,1)}, u32[]{:S(2)}, u32[]{:S(2)}) collective-permute-start(bf16[768,128]{1,0:T(8,128)(2,1)S(1)} %get-tuple-element.6), channel_id=1, source_target_pairs={{0,16},{2,18},{4,20},{6,22},{8,24},{10,26},{12,28},{14,30},{1,17},... | collective-permute-start | bytes 589832 | tf_op jit(solution)/shard_map/ppermute | solution.py:15
  39.5 51.0 %collective-permute-start.5 = (bf16[768,128]{1,0:T(8,128)(2,1)S(1)}, bf16[768,128]{1,0:T(8,128)(2,1)}, u32[]{:S(2)}, u32[]{:S(2)}) collective-permute-start(bf16[768,128]{1,0:T(8,128)(2,1)S(1)} %get-tuple-element.7), channel_id=1, source_target_pairs={{0,14},{2,16},{4,18},{6,20},{8,22},{10,24},{12,26},{14,28},{16,30}... | collective-permute-start | bytes 589832 | tf_op jit(solution)/shard_map/ppermute | solution.py:15
  41.5 48.0 %collective-permute-start.4 = (bf16[768,128]{1,0:T(8,128)(2,1)S(1)}, bf16[768,128]{1,0:T(8,128)(2,1)}, u32[]{:S(2)}, u32[]{:S(2)}) collective-permute-start(bf16[768,128]{1,0:T(8,128)(2,1)S(1)} %get-tuple-element.8), channel_id=1, source_target_pairs={{0,2},{2,4},{4,6},{6,8},{8,10},{10,12},{12,14},{14,16},{16,18},{18... | collective-permute-start | bytes 589832 | tf_op jit(solution)/shard_map/ppermute | solution.py:15
  45.0 18.1 %collective-permute-start = (bf16[768,128]{1,0:T(8,128)(2,1)}, bf16[768,128]{1,0:T(8,128)(2,1)}, u32[]{:S(2)}, u32[]{:S(2)}) collective-permute-start(bf16[768,128]{1,0:T(8,128)(2,1)} %get-tuple-element.12), channel_id=1, source_target_pairs={{18,0},{20,2},{22,4},{24,6},{26,8},{28,10},{30,12},{19,1},{21,3},{... | collective-permute-start | bytes 589832 | tf_op jit(solution)/shard_map/ppermute | solution.py:15
  63.1 27.6 %copy-start.1 = (bf16[1024,128]{1,0:T(8,128)(2,1)S(1)}, bf16[1024,128]{1,0:T(8,128)(2,1)}, u32[]{:S(2)}) copy-start(bf16[1024,128]{1,0:T(8,128)(2,1)} %param.4) | copy-start | bytes 786436
  63.1 10.3 %collective-permute-start.1 = (bf16[768,128]{1,0:T(8,128)(2,1)S(1)}, bf16[768,128]{1,0:T(8,128)(2,1)S(1)}, u32[]{:S(2)}, u32[]{:S(2)}) collective-permute-start(bf16[768,128]{1,0:T(8,128)(2,1)S(1)} %get-tuple-element.11), channel_id=1, source_target_pairs={{16,0},{18,2},{20,4},{22,6},{24,8},{26,10},{28,12},{30,14},{17,1},... | collective-permute-start | bytes 589832 | tf_op jit(solution)/shard_map/ppermute | solution.py:15
  73.4 10.3 %collective-permute-start.2 = (bf16[768,128]{1,0:T(8,128)(2,1)S(1)}, bf16[768,128]{1,0:T(8,128)(2,1)S(1)}, u32[]{:S(2)}, u32[]{:S(2)}) collective-permute-start(bf16[768,128]{1,0:T(8,128)(2,1)S(1)} %get-tuple-element.10), channel_id=1, source_target_pairs={{14,0},{16,2},{18,4},{20,6},{22,8},{24,10},{26,12},{28,14},{30,16}... | collective-permute-start | bytes 589832 | tf_op jit(solution)/shard_map/ppermute | solution.py:15
  83.7 5.7 %collective-permute-start.3 = (bf16[768,128]{1,0:T(8,128)(2,1)S(1)}, bf16[768,128]{1,0:T(8,128)(2,1)S(1)}, u32[]{:S(2)}, u32[]{:S(2)}) collective-permute-start(bf16[768,128]{1,0:T(8,128)(2,1)S(1)} %get-tuple-element.9), channel_id=1, source_target_pairs={{2,0},{4,2},{6,4},{8,6},{10,8},{12,10},{14,12},{16,14},{18,16},{20... | collective-permute-start | bytes 589832 | tf_op jit(solution)/shard_map/ppermute | solution.py:15
Sparse Core Ops, SparseCore 0:
  198.3 20.3 reduce-scatter.1
where the time goes:
time: 229 us; the launch traced here: 227 us
  local copies, waits for them, and re-layouts  120 us (52%)
  waiting for transfers between devices  57.1 us (25%)
  starting transfers between devices  18.6 us (8%)
  between operations  13.6 us (6%)
  other arithmetic  12.4 us (5%)
  matrix products  5.27 us (2%)
    gather x1, local copies, waits for them, and re-layouts, local(): picked = table[gather_map]  94.8 us
    ppermute x8, waiting for transfers between devices, shifted(): lax.ppermute(value, axis, [(source, source + steps) for source in range(f...  36.6 us
    gather x1, local copies, waits for them, and re-layouts, local(): outgoing = padded[send_rows[0]]  22.3 us
    reduce_scatter x1, waiting for transfers between devices, local(): lax.psum_scatter(partial_value, 'chan', scatter_dimension=1, tiled=True)  20.5 us
    ppermute x8, starting transfers between devices, shifted(): lax.ppermute(value, axis, [(source, source + steps) for source in range(f...  18.6 us
    concatenate x1, other arithmetic, local(): jnp.concatenate([features, received.reshape(8 * slots, group_width), jnp....  7.34 us
    dot_general x1, matrix products, local(): jnp.einsum('kvc,kco->vo', picked, weights, preferred_element_type=jnp.flo...  5.27 us
  transfers between devices with their start and end apart: 9, of which 5 were waited for; matrix products, arithmetic and copies ran while one was open for 1% of the time, Pallas kernels for 0%

commit v1 on v0

v1 whole, which is shorter than its diff:
```python
import functools

import jax
import jax.numpy as jnp
from jax import lax
from jax.experimental import pallas as pl
from jax.experimental.pallas import tpu as pltpu
from jax.sharding import PartitionSpec as P

GRID_COLS = 8
MESH = pl.DeviceIdType.MESH
DIRECTIONS = [(-1, -1), (-1, 0), (-1, 1), (0, -1), (0, 1), (1, -1), (1, 0), (1, 1)]
VERTICAL = {1: (0, 2), 6: (5, 7)}
HORIZONTAL = (3, 4)
LANES = 128
PIECES = 4
CHUNK = 256


def kernel(
    grid_rows, paired, feat, weights, send_rows, gmap, out,
    blocks, rows, lut, table, idx, idx_s, buf_a, buf_b, acc, own, outgoing, incoming,
    blk_send, blk_recv, row_send, row_recv, idx_sem, part_send, part_recv,
):
    voxels = feat.shape[0]
    offsets = gmap.shape[0]
    slot_tiles = rows.shape[1]
    zero_row = 9 * voxels
    piece = voxels // PIECES
    me = lax.axis_index("space")
    chan = lax.axis_index("chan")
    my_row = me // GRID_COLS
    my_col = me % GRID_COLS

    def inside(dx, dy):
        row, col = my_row + dx, my_col + dy
        return (row >= 0) & (row < grid_rows) & (col >= 0) & (col < GRID_COLS)

    def device(dx, dy):
        return (me + dx * GRID_COLS + dy, chan)

    def block_copy(src, slot, part, dx, dy):
        return pltpu.make_async_remote_copy(
            src_ref=src.at[pl.ds(part * piece, piece)],
            dst_ref=blocks.at[slot, pl.ds(part * piece, piece)],
            send_sem=blk_send.at[slot, part],
            recv_sem=blk_recv.at[slot, part],
            device_id=device(dx, dy),
            device_id_type=MESH,
        )

    def rows_copy(slot, dx, dy):
        return pltpu.make_async_remote_copy(
            src_ref=send_rows.at[slot],
            dst_ref=rows.at[slot],
            send_sem=row_send.at[slot],
            recv_sem=row_recv.at[slot],
            device_id=device(dx, dy),
            device_id_type=MESH,
        )

    rows[...] = jnp.full(rows.shape, voxels, jnp.int32)

    barrier = pltpu.get_barrier_semaphore()
    expected = jnp.int32(1 if paired else 0)
    for dx, dy in DIRECTIONS:
        expected = expected + inside(dx, dy).astype(jnp.int32)

        @pl.when(inside(dx, dy))
        def _():
            pl.semaphore_signal(barrier, inc=1, device_id=device(dx, dy), device_id_type=MESH)

    if paired:
        pl.semaphore_signal(barrier, inc=1, device_id=(me, 1 - chan), device_id_type=MESH)
    pl.semaphore_wait(barrier, expected)

    for part in range(PIECES):
        for slot in VERTICAL:
            dx, dy = DIRECTIONS[slot]

            @pl.when(inside(dx, dy))
            def _():
                if part == 0:
                    rows_copy(slot, dx, dy).start()
                block_copy(feat, slot, part, dx, dy).start()

    for slot, (dx, dy) in enumerate(DIRECTIONS):
        if slot in VERTICAL:
            continue

        @pl.when(inside(dx, dy))
        def _():
            rows_copy(slot, dx, dy).start()
            if slot in HORIZONTAL:
                for part in range(PIECES):
                    block_copy(feat, slot, part, dx, dy).start()

    def widen(src, number, part):
        table[pl.ds(number * voxels + part * piece, piece), :] = src[pl.ds(part * piece, piece), :].astype(jnp.float32)

    table[pl.ds(zero_row, 8), :] = jnp.zeros((8, LANES), jnp.float32)
    for part in range(PIECES):
        widen(feat, 0, part)

    for slot, (dx, dy) in enumerate(DIRECTIONS):
        @pl.when(inside(-dx, -dy))
        def _():
            rows_copy(slot, -dx, -dy).wait_recv()

        entry = rows[slot]
        lut[slot] = jnp.where(entry < voxels, entry + (1 + slot) * voxels, zero_row)

    own_tiles = voxels // LANES

    def compose(col, _):
        lanes = pl.ds(pl.multiple_of(col * LANES, LANES), LANES)
        starts = list(range(0, offsets - 7, 8))
        if offsets % 8:
            starts.append(offsets - 8)
        entries = [gmap[pl.ds(start, 8), lanes] for start in starts]
        within = [entry & (LANES - 1) for entry in entries]
        tiles = [entry >> 7 for entry in entries]
        result = [jnp.where(entry < voxels, entry, zero_row) for entry in entries]
        for slot in range(8):
            for tile in range(slot_tiles):
                line = jnp.broadcast_to(lut[slot, pl.ds(tile, 1), :], (8, LANES))
                number = own_tiles + slot * slot_tiles + tile
                for i in range(len(starts)):
                    found = jnp.take_along_axis(line, within[i], axis=1, mode="promise_in_bounds")
                    result[i] = jnp.where(tiles[i] == number, found, result[i])
        for start, value in zip(starts, result):
            idx[pl.ds(start, 8), lanes] = value
        return 0

    lax.fori_loop(0, own_tiles, compose, 0)
    to_scalar = pltpu.make_async_copy(idx, idx_s, idx_sem)
    to_scalar.start()

    for part in range(PIECES):
        for slot, (left, right) in VERTICAL.items():
            dx, dy = DIRECTIONS[slot]

            @pl.when(inside(-dx, -dy))
            def _():
                block_copy(feat, slot, part, -dx, -dy).wait_recv()
                for target, step in ((left, -1), (right, 1)):
                    @pl.when(inside(0, step))
                    def _():
                        block_copy(blocks.at[slot], target, part, 0, step).start()

                widen(blocks.at[slot], 1 + slot, part)

    for slot in HORIZONTAL + (0, 2, 5, 7):
        dx, dy = DIRECTIONS[slot]

        @pl.when(inside(-dx, -dy))
        def _():
            for part in range(PIECES):
                block_copy(feat, slot, part, -dx, -dy).wait_recv()
                widen(blocks.at[slot], 1 + slot, part)

    to_scalar.wait()

    def gather(buf, first, count, base):
        for half in range(count):
            for v in range(CHUNK):
                row = idx_s[first + half, base + v]
                buf[pl.ds(v, 1), pl.ds(half * LANES, LANES)] = table[pl.ds(row, 1), :]

    def product(buf, pair, base):
        kernel_pair = weights[pl.ds(2 * pair, 2)].reshape(2 * LANES, weights.shape[2])
        acc[...] += jnp.dot(buf[...].astype(jnp.bfloat16), kernel_pair, preferred_element_type=jnp.float32)

    pairs = offsets // 2
    other = pl.ds(pl.multiple_of((1 - chan) * LANES, LANES), LANES)
    mine = pl.ds(pl.multiple_of(chan * LANES, LANES), LANES)

    def partial_copy(chunk):
        span = pl.ds(pl.multiple_of(chunk * CHUNK, CHUNK), CHUNK)
        return pltpu.make_async_remote_copy(
            src_ref=outgoing.at[span],
            dst_ref=incoming.at[span],
            send_sem=part_send.at[chunk],
            recv_sem=part_recv.at[chunk],
            device_id=(me, 1 - chan),
            device_id_type=MESH,
        )

    def step(chunk, _):
        base = chunk * CHUNK
        span = pl.ds(pl.multiple_of(base, CHUNK), CHUNK)
        acc[...] = jnp.zeros_like(acc)
        gather(buf_a, 0, 2, base)

        def two(i, _):
            product(buf_a, 2 * i, base)
            gather(buf_b, 4 * i + 2, 2, base)
            product(buf_b, 2 * i + 1, base)
            gather(buf_a, 4 * i + 4, 2, base)
            return 0

        lax.fori_loop(0, (pairs - 1) // 2, two, 0)
        product(buf_a, pairs - 1, base)
        gather(buf_b, offsets - 1, 1, base)
        total = acc[...] + jnp.dot(
            buf_b[:, pl.ds(0, LANES)].astype(jnp.bfloat16), weights[offsets - 1], preferred_element_type=jnp.float32
        )
        if not paired:
            out[span, :] = total
            return 0
        acc[...] = total
        own[span, :] = acc[:, mine]
        outgoing[span, :] = acc[:, other]
        partial_copy(chunk).start()
        return 0

    chunks = voxels // CHUNK
    lax.fori_loop(0, chunks, step, 0)

    def finish(chunk, _):
        span = pl.ds(pl.multiple_of(chunk * CHUNK, CHUNK), CHUNK)
        partial_copy(chunk).wait()
        out[span, :] = (own[span, :] + incoming[span, :]).astype(out.dtype)
        return 0

    if paired:
        lax.fori_loop(0, chunks, finish, 0)

    for slot, (dx, dy) in enumerate(DIRECTIONS):
        @pl.when(inside(dx, dy))
        def _():
            rows_copy(slot, dx, dy).wait_send()
            if slot in VERTICAL or slot in HORIZONTAL:
                for part in range(PIECES):
                    block_copy(feat, slot, part, dx, dy).wait_send()

    for slot, targets in VERTICAL.items():
        dx, dy = DIRECTIONS[slot]
        for target, step_y in zip(targets, (-1, 1)):
            @pl.when(inside(-dx, -dy) & inside(0, step_y))
            def _():
                for part in range(PIECES):
                    block_copy(feat, target, part, 0, step_y).wait_send()


def local(grid_rows, features, weights, send_rows, gather_map):
    voxels, own_width = features.shape
    offsets = gather_map.shape[0]
    out_width = weights.shape[2]
    slots = send_rows.shape[2]
    lines = send_rows.reshape(8, slots // LANES, LANES)
    paired = lax.axis_size("chan") == 2 and own_width == LANES
    if not paired:
        features = jnp.pad(features, ((0, 0), (0, LANES - own_width)))
        weights = jnp.pad(weights, ((0, 0), (0, LANES - own_width), (0, 0)))
    width = LANES
    chunks = voxels // CHUNK
    dma = pltpu.SemaphoreType.DMA
    result = jax.ShapeDtypeStruct((voxels, width) if paired else (voxels, out_width), jnp.bfloat16 if paired else jnp.float32)
    made = pl.pallas_call(
        functools.partial(kernel, grid_rows, paired),
        out_shape=result,
        in_specs=[pl.BlockSpec(memory_space=pltpu.VMEM)] * 4,
        out_specs=pl.BlockSpec(memory_space=pltpu.VMEM),
        scratch_shapes=[
            pltpu.VMEM((8, voxels, width), jnp.bfloat16),
            pltpu.VMEM(lines.shape, jnp.int32),
            pltpu.VMEM(lines.shape, jnp.int32),
            pltpu.VMEM((9 * voxels + 8, width), jnp.float32),
            pltpu.VMEM((offsets, voxels), jnp.int32),
            pltpu.SMEM((offsets, voxels), jnp.int32),
            pltpu.VMEM((CHUNK, 2 * width), jnp.float32),
            pltpu.VMEM((CHUNK, 2 * width), jnp.float32),
            pltpu.VMEM((CHUNK, out_width), jnp.float32),
            pltpu.VMEM((voxels, width), jnp.float32),
            pltpu.VMEM((voxels, width), jnp.float32),
            pltpu.VMEM((voxels, width), jnp.float32),
            dma((8, PIECES)), dma((8, PIECES)), dma((8,)), dma((8,)), dma, dma((chunks,)), dma((chunks,)),
        ],
        compiler_params=pltpu.CompilerParams(
            collective_id=0, has_side_effects=True, vmem_limit_bytes=40 * 1024 * 1024
        ),
        cost_estimate=pl.CostEstimate(
            flops=2 * voxels * offsets * width * out_width, bytes_accessed=6 * 1024 * 1024, transcendentals=0
        ),
    )(features, weights, lines, gather_map)
    if paired:
        return made
    return lax.psum_scatter(made, "chan", scatter_dimension=1, tiled=True).astype(jnp.bfloat16)


def solution(mesh):
    grid_rows = mesh.shape["space"] // GRID_COLS
    in_specs = (P("space", "chan"), P(None, "chan", None), P("space", None, None), P(None, "space"))
    out_specs = P("space", "chan")
    return jax.shard_map(
        functools.partial(local, grid_rows), mesh=mesh, in_specs=in_specs, out_specs=out_specs, check_vma=False
    )
```

time: 229 us -> 99.3 us (0.43)
  local copies, waits for them, and re-layouts: 120 us -> 4.78 us
  Pallas kernels: 0 us -> 94.2 us
  waiting for transfers between devices: 57.1 us -> 0 us
  starting transfers between devices: 18.6 us -> 0 us
  between operations: 13.6 us -> 0.02 us
  other arithmetic: 12.4 us -> 0 us
  matrix products: 5.27 us -> 0 us
    gather x2 -> x0, local copies, waits for them, and re-layouts: 117 us -> none  [the longest x1 94.8 us: local(): picked = table[gather_map]]
    pallas_call x0 -> x1, Pallas kernels: none -> 94.2 us  [local(): pl.pallas_call(functools.partial(kernel, grid_rows, paired), out_shape=re...]
    ppermute x8 -> x0, waiting for transfers between devices: 36.6 us -> none  [shifted(): lax.ppermute(value, axis, [(source, source + steps) for source in range(f...]
    reduce_scatter x1 -> x0, waiting for transfers between devices: 20.5 us -> none  [local(): lax.psum_scatter(partial_value, 'chan', scatter_dimension=1, tiled=True)]
    ppermute x8 -> x0, starting transfers between devices: 18.6 us -> none  [shifted(): lax.ppermute(value, axis, [(source, source + steps) for source in range(f...]
    concatenate x1 -> x0, other arithmetic: 7.34 us -> none  [local(): jnp.concatenate([features, received.reshape(8 * slots, group_width), jnp....]
    dot_general x1 -> x0, matrix products: 5.27 us -> none  [local(): jnp.einsum('kvc,kco->vo', picked, weights, preferred_element_type=jnp.flo...]
    unnamed x6 -> x7, local copies, waits for them, and re-layouts: 0.01 us -> 4.03 us
  transfers between devices with their start and end apart: 9 -> 0, of which waited for: 5 -> 0; matrix products, arithmetic and copies ran while one was open for 1% -> 0% of each run, Pallas kernels for 0% -> 0%
where the time goes in v1:
time: 99.3 us; the launch traced here: 99 us
  Pallas kernels  94.2 us (95%)
  local copies, waits for them, and re-layouts  4.78 us (5%)
    pallas_call x1, Pallas kernels, local(): pl.pallas_call(functools.partial(kernel, grid_rows, paired), out_shape=re...  94.2 us
    unnamed x7, local copies, waits for them, and re-layouts  4.03 us

profile of v1, /device:TPU:2, one launch (start us, length us, event | category | flops | bytes accessed | tf_op | source)
XLA Modules:
  0.0 99.0 jit_solution(16354654772021631669)
XLA Ops:
  0.0 0.7 copy.5.send_rows
  0.7 0.0 copy-start
  0.8 1.5 %copy-done = bf16[27,128,256]{2,1,0:T(8,128)(2,1)S(1)} copy-done((bf16[27,128,256]{2,1,0:T(8,128)(2,1)S(1)}, bf16[27,128,256]{2,1,0:T(8,128)(2,1)}, u32[]{:S(2)}) %copy-start) | copy-done | bytes 1769496
  2.2 0.0 copy-start.1
  2.2 0.9 copy-done.1
  3.2 0.0 copy-start.2
  3.2 0.9 copy-done.2
  4.1 94.2 %shard_map.46 = bf16[1024,128]{1,0:T(8,128)(2,1)S(1)} custom-call(bf16[1024,128]{1,0:T(8,128)(2,1)S(1)} %copy-done.1, bf16[27,128,256]{2,1,0:T(8,128)(2,1)S(1)} %copy-done, s32[8,6,128]{2,1,0:T(8,128)S(1)} %copy.5.send_rows, s32[27,1024]{1,0:T(8,128)S(1)} %copy-done.2), custom_call_target="tpu_custom_call" | custom-call | flops 1811939328 | bytes 6291456 | tf_op jit(solution)/shard_map/pallas_call | solution.py:260
  98.3 0.7 copy.7
Async XLA Ops:
  0.7 1.5 %copy-start = (bf16[27,128,256]{2,1,0:T(8,128)(2,1)S(1)}, bf16[27,128,256]{2,1,0:T(8,128)(2,1)}, u32[]{:S(2)}) copy-start(bf16[27,128,256]{2,1,0:T(8,128)(2,1)} %weights.1) | copy-start | bytes 5308420
  2.2 0.9 copy-start.1
  3.2 0.9 copy-start.2

commit v2 on v1

--- a/solution.py
+++ b/solution.py
@@ -15,16 +15,17 @@
 LANES = 128
 PIECES = 4
 CHUNK = 256
+GROUP = 32
 
 
 def kernel(
-    grid_rows, paired, feat, weights, send_rows, gmap, out,
-    blocks, rows, lut, table, idx, idx_s, buf_a, buf_b, acc, own, outgoing, incoming,
-    blk_send, blk_recv, row_send, row_recv, idx_sem, part_send, part_recv,
+    grid_rows, paired, feat_hbm, weights_hbm, send_rows, gmap_hbm, out,
+    feat, weights, gmap, blocks, rows, lut, table, idx, idx_s, buf_a, buf_b, acc, own, outgoing, incoming,
+    blk_send, blk_recv, row_send, row_recv, in_sem, idx_sem, part_send, part_recv,
 ):
     voxels = feat.shape[0]
     offsets = gmap.shape[0]
-    slot_tiles = rows.shape[1]
+    slot_tiles = rows.shape[2] // LANES
     zero_row = 9 * voxels
     piece = voxels // PIECES
     me = lax.axis_index("space")
@@ -51,7 +52,7 @@
 
     def rows_copy(slot, dx, dy):
         return pltpu.make_async_remote_copy(
-            src_ref=send_rows.at[slot],
+            src_ref=send_rows.at[0, pl.ds(slot, 1)],
             dst_ref=rows.at[slot],
             send_sem=row_send.at[slot],
             recv_sem=row_recv.at[slot],
@@ -59,6 +60,13 @@
             device_id_type=MESH,
         )
 
+    staged = [
+        pltpu.make_async_copy(source, target, in_sem.at[number])
+        for number, (source, target) in enumerate(((feat_hbm, feat), (gmap_hbm, gmap), (weights_hbm, weights)))
+    ]
+    for copy in staged:
+        copy.start()
+
     rows[...] = jnp.full(rows.shape, voxels, jnp.int32)
 
     barrier = pltpu.get_barrier_semaphore()
@@ -82,7 +90,7 @@
             def _():
                 if part == 0:
                     rows_copy(slot, dx, dy).start()
-                block_copy(feat, slot, part, dx, dy).start()
+                block_copy(feat_hbm, slot, part, dx, dy).start()
 
     for slot, (dx, dy) in enumerate(DIRECTIONS):
         if slot in VERTICAL:
@@ -93,14 +101,16 @@
             rows_copy(slot, dx, dy).start()
             if slot in HORIZONTAL:
                 for part in range(PIECES):
-                    block_copy(feat, slot, part, dx, dy).start()
+                    block_copy(feat_hbm, slot, part, dx, dy).start()
 
     def widen(src, number, part):
         table[pl.ds(number * voxels + part * piece, piece), :] = src[pl.ds(part * piece, piece), :].astype(jnp.float32)
 
     table[pl.ds(zero_row, 8), :] = jnp.zeros((8, LANES), jnp.float32)
+    staged[0].wait()
     for part in range(PIECES):
         widen(feat, 0, part)
+    staged[1].wait()
 
     for slot, (dx, dy) in enumerate(DIRECTIONS):
         @pl.when(inside(-dx, -dy))
@@ -123,7 +133,7 @@
         result = [jnp.where(entry < voxels, entry, zero_row) for entry in entries]
         for slot in range(8):
             for tile in range(slot_tiles):
-                line = jnp.broadcast_to(lut[slot, pl.ds(tile, 1), :], (8, LANES))
+                line = jnp.broadcast_to(lut[slot, :, pl.ds(tile * LANES, LANES)], (8, LANES))
                 number = own_tiles + slot * slot_tiles + tile
                 for i in range(len(starts)):
                     found = jnp.take_along_axis(line, within[i], axis=1, mode="promise_in_bounds")
@@ -160,18 +170,26 @@
                 widen(blocks.at[slot], 1 + slot, part)
 
     to_scalar.wait()
-
-    def gather(buf, first, count, base):
-        for half in range(count):
-            for v in range(CHUNK):
-                row = idx_s[first + half, base + v]
-                buf[pl.ds(v, 1), pl.ds(half * LANES, LANES)] = table[pl.ds(row, 1), :]
-
-    def product(buf, pair, base):
-        kernel_pair = weights[pl.ds(2 * pair, 2)].reshape(2 * LANES, weights.shape[2])
+    staged[2].wait()
+
+    centre = offsets // 2
+    pairs = centre
+
+    def offset_of(number):
+        return number + (number >= centre).astype(jnp.int32)
+
+    def gather(buf, pair, base):
+        for half in range(2):
+            offset = offset_of(2 * pair + half)
+            for first in range(0, CHUNK, GROUP):
+                taken = [table[pl.ds(idx_s[offset, base + first + v], 1), :] for v in range(GROUP)]
+                for v in range(GROUP):
+                    buf[pl.ds(first + v, 1), pl.ds(half * LANES, LANES)] = taken[v]
+
+    def product(buf, pair):
+        kernel_pair = jnp.concatenate([weights[offset_of(2 * pair)], weights[offset_of(2 * pair + 1)]], axis=0)
         acc[...] += jnp.dot(buf[...].astype(jnp.bfloat16), kernel_pair, preferred_element_type=jnp.float32)
 
-    pairs = offsets // 2
     other = pl.ds(pl.multiple_of((1 - chan) * LANES, LANES), LANES)
     mine = pl.ds(pl.multiple_of(chan * LANES, LANES), LANES)
 
@@ -189,26 +207,21 @@
     def step(chunk, _):
         base = chunk * CHUNK
         span = pl.ds(pl.multiple_of(base, CHUNK), CHUNK)
-        acc[...] = jnp.zeros_like(acc)
-        gather(buf_a, 0, 2, base)
+        acc[...] = jnp.dot(feat[span, :], weights[centre], preferred_element_type=jnp.float32)
+        gather(buf_a, jnp.int32(0), base)
 
         def two(i, _):
-            product(buf_a, 2 * i, base)
-            gather(buf_b, 4 * i + 2, 2, base)
-            product(buf_b, 2 * i + 1, base)
-            gather(buf_a, 4 * i + 4, 2, base)
+            product(buf_a, 2 * i)
+            gather(buf_b, 2 * i + 1, base)
+            product(buf_b, 2 * i + 1)
+            gather(buf_a, 2 * i + 2, base)
             return 0
 
         lax.fori_loop(0, (pairs - 1) // 2, two, 0)
-        product(buf_a, pairs - 1, base)
-        gather(buf_b, offsets - 1, 1, base)
-        total = acc[...] + jnp.dot(
-            buf_b[:, pl.ds(0, LANES)].astype(jnp.bfloat16), weights[offsets - 1], preferred_element_type=jnp.float32
-        )
+        product(buf_a, jnp.int32(pairs - 1))
         if not paired:
-            out[span, :] = total
+            out[span, :] = acc[...]
             return 0
-        acc[...] = total
         own[span, :] = acc[:, mine]
         outgoing[span, :] = acc[:, other]
         partial_copy(chunk).start()
@@ -248,7 +261,6 @@
     offsets = gather_map.shape[0]
     out_width = weights.shape[2]
     slots = send_rows.shape[2]
-    lines = send_rows.reshape(8, slots // LANES, LANES)
     paired = lax.axis_size("chan") == 2 and own_width == LANES
     if not paired:
         features = jnp.pad(features, ((0, 0), (0, LANES - own_width)))
@@ -260,12 +272,15 @@
     made = pl.pallas_call(
         functools.partial(kernel, grid_rows, paired),
         out_shape=result,
-        in_specs=[pl.BlockSpec(memory_space=pltpu.VMEM)] * 4,
+        in_specs=[pl.BlockSpec(memory_space=pl.ANY)] * 4,
         out_specs=pl.BlockSpec(memory_space=pltpu.VMEM),
         scratch_shapes=[
+            pltpu.VMEM(features.shape, features.dtype),
+            pltpu.VMEM(weights.shape, weights.dtype),
+            pltpu.VMEM(gather_map.shape, gather_map.dtype),
             pltpu.VMEM((8, voxels, width), jnp.bfloat16),
-            pltpu.VMEM(lines.shape, jnp.int32),
-            pltpu.VMEM(lines.shape, jnp.int32),
+            pltpu.VMEM((8, 1, slots), jnp.int32),
+            pltpu.VMEM((8, 1, slots), jnp.int32),
             pltpu.VMEM((9 * voxels + 8, width), jnp.float32),
             pltpu.VMEM((offsets, voxels), jnp.int32),
             pltpu.SMEM((offsets, voxels), jnp.int32),
@@ -275,7 +290,7 @@
             pltpu.VMEM((voxels, width), jnp.float32),
             pltpu.VMEM((voxels, width), jnp.float32),
             pltpu.VMEM((voxels, width), jnp.float32),
-            dma((8, PIECES)), dma((8, PIECES)), dma((8,)), dma((8,)), dma, dma((chunks,)), dma((chunks,)),
+            dma((8, PIECES)), dma((8, PIECES)), dma((8,)), dma((8,)), dma((3,)), dma, dma((chunks,)), dma((chunks,)),
         ],
         compiler_params=pltpu.CompilerParams(
             collective_id=0, has_side_effects=True, vmem_limit_bytes=40 * 1024 * 1024
@@ -283,7 +298,7 @@
         cost_estimate=pl.CostEstimate(
             flops=2 * voxels * offsets * width * out_width, bytes_accessed=6 * 1024 * 1024, transcendentals=0
         ),
-    )(features, weights, lines, gather_map)
+    )(features, weights, send_rows, gather_map)
     if paired:
         return made
     return lax.psum_scatter(made, "chan", scatter_dimension=1, tiled=True).astype(jnp.bfloat16)

time: 99.3 us -> 98.7 us (level)
    unnamed x7 -> x9, local copies, waits for them, and re-layouts: 4.03 us -> 4.77 us
where the time goes in v2:
time: 98.7 us; the launch traced here: 98.5 us
  Pallas kernels  93.7 us (95%)
  local copies, waits for them, and re-layouts  4.77 us (5%)
    pallas_call x1, Pallas kernels, local(): pl.pallas_call(functools.partial(kernel, grid_rows, paired), out_shape=re...  93.7 us
    unnamed x9, local copies, waits for them, and re-layouts  4.77 us

profile of v2, /device:TPU:2, one launch (start us, length us, event | category | flops | bytes accessed | tf_op | source)
XLA Modules:
  0.0 98.5 jit_solution(5117836939616887858)
XLA Ops:
  0.0 0.0 copy-start
  0.0 1.5 %copy-done = bf16[27,128,256]{2,1,0:T(8,128)(2,1)S(1)} copy-done((bf16[27,128,256]{2,1,0:T(8,128)(2,1)S(1)}, bf16[27,128,256]{2,1,0:T(8,128)(2,1)}, u32[]{:S(2)}) %copy-start) | copy-done | bytes 1769496
  1.5 0.0 copy-start.1
  1.5 0.9 copy-done.1
  2.4 0.0 copy-start.2
  2.4 0.9 copy-done.2
  3.3 0.0 copy-start.3
  3.3 0.7 copy-done.3
  4.1 93.7 %shard_map.46 = bf16[1024,128]{1,0:T(8,128)(2,1)S(1)} custom-call(bf16[1024,128]{1,0:T(8,128)(2,1)S(1)} %copy-done.1, bf16[27,128,256]{2,1,0:T(8,128)(2,1)S(1)} %copy-done, s32[1,8,768]{2,1,0:T(8,128)S(1)} %copy-done.3, s32[27,1024]{1,0:T(8,128)S(1)} %copy-done.2), custom_call_target="tpu_custom_call" | custom-call | flops 1811939328 | bytes 6291456 | tf_op jit(solution)/shard_map/pallas_call | solution.py:272
  97.8 0.7 copy.6
Async XLA Ops:
  0.0 1.5 %copy-start = (bf16[27,128,256]{2,1,0:T(8,128)(2,1)S(1)}, bf16[27,128,256]{2,1,0:T(8,128)(2,1)}, u32[]{:S(2)}) copy-start(bf16[27,128,256]{2,1,0:T(8,128)(2,1)} %weights_hbm.1) | copy-start | bytes 5308420
  1.5 0.9 copy-start.1
  2.4 0.9 copy-start.2
  3.3 0.7 copy-start.3

commit v3 on v2

--- a/solution.py
+++ b/solution.py
@@ -18,10 +18,9 @@
 GROUP = 32
 
 
-def kernel(
-    grid_rows, paired, feat_hbm, weights_hbm, send_rows, gmap_hbm, out,
-    feat, weights, gmap, blocks, rows, lut, table, idx, idx_s, buf_a, buf_b, acc, own, outgoing, incoming,
-    blk_send, blk_recv, row_send, row_recv, in_sem, idx_sem, part_send, part_recv,
+def exchange(
+    grid_rows, feat, send_rows, gmap, table, idx,
+    blocks, rows, lut, blk_send, blk_recv, row_send, row_recv,
 ):
     voxels = feat.shape[0]
     offsets = gmap.shape[0]
@@ -60,17 +59,10 @@
             device_id_type=MESH,
         )
 
-    staged = [
-        pltpu.make_async_copy(source, target, in_sem.at[number])
-        for number, (source, target) in enumerate(((feat_hbm, feat), (gmap_hbm, gmap), (weights_hbm, weights)))
-    ]
-    for copy in staged:
-        copy.start()
-
     rows[...] = jnp.full(rows.shape, voxels, jnp.int32)
 
     barrier = pltpu.get_barrier_semaphore()
-    expected = jnp.int32(1 if paired else 0)
+    expected = jnp.int32(0)
     for dx, dy in DIRECTIONS:
         expected = expected + inside(dx, dy).astype(jnp.int32)
 
@@ -78,8 +70,6 @@
         def _():
             pl.semaphore_signal(barrier, inc=1, device_id=device(dx, dy), device_id_type=MESH)
 
-    if paired:
-        pl.semaphore_signal(barrier, inc=1, device_id=(me, 1 - chan), device_id_type=MESH)
     pl.semaphore_wait(barrier, expected)
 
     for part in range(PIECES):
@@ -90,7 +80,7 @@
             def _():
                 if part == 0:
                     rows_copy(slot, dx, dy).start()
-                block_copy(feat_hbm, slot, part, dx, dy).start()
+                block_copy(feat, slot, part, dx, dy).start()
 
     for slot, (dx, dy) in enumerate(DIRECTIONS):
         if slot in VERTICAL:
@@ -101,16 +91,14 @@
             rows_copy(slot, dx, dy).start()
             if slot in HORIZONTAL:
                 for part in range(PIECES):
-                    block_copy(feat_hbm, slot, part, dx, dy).start()
+                    block_copy(feat, slot, part, dx, dy).start()
 
     def widen(src, number, part):
         table[pl.ds(number * voxels + part * piece, piece), :] = src[pl.ds(part * piece, piece), :].astype(jnp.float32)
 
     table[pl.ds(zero_row, 8), :] = jnp.zeros((8, LANES), jnp.float32)
-    staged[0].wait()
     for part in range(PIECES):
         widen(feat, 0, part)
-    staged[1].wait()
 
     for slot, (dx, dy) in enumerate(DIRECTIONS):
         @pl.when(inside(-dx, -dy))
@@ -143,8 +131,6 @@
         return 0
 
     lax.fori_loop(0, own_tiles, compose, 0)
-    to_scalar = pltpu.make_async_copy(idx, idx_s, idx_sem)
-    to_scalar.start()
 
     for part in range(PIECES):
         for slot, (left, right) in VERTICAL.items():
@@ -169,8 +155,35 @@
                 block_copy(feat, slot, part, -dx, -dy).wait_recv()
                 widen(blocks.at[slot], 1 + slot, part)
 
+    for slot, (dx, dy) in enumerate(DIRECTIONS):
+        @pl.when(inside(dx, dy))
+        def _():
+            rows_copy(slot, dx, dy).wait_send()
+            if slot in VERTICAL or slot in HORIZONTAL:
+                for part in range(PIECES):
+                    block_copy(feat, slot, part, dx, dy).wait_send()
+
+    for slot, targets in VERTICAL.items():
+        dx, dy = DIRECTIONS[slot]
+        for target, step_y in zip(targets, (-1, 1)):
+            @pl.when(inside(-dx, -dy) & inside(0, step_y))
+            def _():
+                for part in range(PIECES):
+                    block_copy(feat, target, part, 0, step_y).wait_send()
+
+
+def convolve(paired, table, idx, feat, weights, out, idx_s, buf_a, buf_b, acc, own, outgoing, incoming, idx_sem, part_send, part_recv):
+    voxels = feat.shape[0]
+    offsets = weights.shape[0]
+    me = lax.axis_index("space")
+    chan = lax.axis_index("chan")
+    to_scalar = pltpu.make_async_copy(idx, idx_s, idx_sem)
+    to_scalar.start()
+    if paired:
+        barrier = pltpu.get_barrier_semaphore()
+        pl.semaphore_signal(barrier, inc=1, device_id=(me, 1 - chan), device_id_type=MESH)
+        pl.semaphore_wait(barrier, 1)
     to_scalar.wait()
-    staged[2].wait()
 
     centre = offsets // 2
     pairs = centre
@@ -182,7 +195,7 @@
         for half in range(2):
             offset = offset_of(2 * pair + half)
             for first in range(0, CHUNK, GROUP):
-                taken = [table[pl.ds(idx_s[offset, base + first + v], 1), :] for v in range(GROUP)]
+                taken = [table[idx_s[offset, base + first + v]] for v in range(GROUP)]
                 for v in range(GROUP):
                     buf[pl.ds(first + v, 1), pl.ds(half * LANES, LANES)] = taken[v]
 
@@ -238,22 +251,6 @@
 
     if paired:
         lax.fori_loop(0, chunks, finish, 0)
-
-    for slot, (dx, dy) in enumerate(DIRECTIONS):
-        @pl.when(inside(dx, dy))
-        def _():
-            rows_copy(slot, dx, dy).wait_send()
-            if slot in VERTICAL or slot in HORIZONTAL:
-                for part in range(PIECES):
-                    block_copy(feat, slot, part, dx, dy).wait_send()
-
-    for slot, targets in VERTICAL.items():
-        dx, dy = DIRECTIONS[slot]
-        for target, step_y in zip(targets, (-1, 1)):
-            @pl.when(inside(-dx, -dy) & inside(0, step_y))
-            def _():
-                for part in range(PIECES):
-                    block_copy(feat, target, part, 0, step_y).wait_send()
 
 
 def local(grid_rows, features, weights, send_rows, gather_map):
@@ -269,20 +266,32 @@
     chunks = voxels // CHUNK
     dma = pltpu.SemaphoreType.DMA
     result = jax.ShapeDtypeStruct((voxels, width) if paired else (voxels, out_width), jnp.bfloat16 if paired else jnp.float32)
-    made = pl.pallas_call(
-        functools.partial(kernel, grid_rows, paired),
-        out_shape=result,
-        in_specs=[pl.BlockSpec(memory_space=pl.ANY)] * 4,
-        out_specs=pl.BlockSpec(memory_space=pltpu.VMEM),
+    vmem = pl.BlockSpec(memory_space=pltpu.VMEM)
+    table, idx = pl.pallas_call(
+        functools.partial(exchange, grid_rows),
+        out_shape=(
+            jax.ShapeDtypeStruct((9 * voxels + 8, width), jnp.float32),
+            jax.ShapeDtypeStruct((offsets, voxels), jnp.int32),
+        ),
+        in_specs=[vmem] * 3,
+        out_specs=(vmem, vmem),
         scratch_shapes=[
-            pltpu.VMEM(features.shape, features.dtype),
-            pltpu.VMEM(weights.shape, weights.dtype),
-            pltpu.VMEM(gather_map.shape, gather_map.dtype),
             pltpu.VMEM((8, voxels, width), jnp.bfloat16),
             pltpu.VMEM((8, 1, slots), jnp.int32),
             pltpu.VMEM((8, 1, slots), jnp.int32),
-            pltpu.VMEM((9 * voxels + 8, width), jnp.float32),
-            pltpu.VMEM((offsets, voxels), jnp.int32),
+            dma((8, PIECES)), dma((8, PIECES)), dma((8,)), dma((8,)),
+        ],
+        compiler_params=pltpu.CompilerParams(
+            collective_id=0, has_side_effects=True, vmem_limit_bytes=20 * 1024 * 1024
+        ),
+        cost_estimate=pl.CostEstimate(flops=0, bytes_accessed=64 * 1024 * 1024, transcendentals=0),
+    )(features, send_rows, gather_map)
+    made = pl.pallas_call(
+        functools.partial(convolve, paired),
+        out_shape=result,
+        in_specs=[vmem] * 4,
+        out_specs=vmem,
+        scratch_shapes=[
             pltpu.SMEM((offsets, voxels), jnp.int32),
             pltpu.VMEM((CHUNK, 2 * width), jnp.float32),
             pltpu.VMEM((CHUNK, 2 * width), jnp.float32),
@@ -290,15 +299,15 @@
             pltpu.VMEM((voxels, width), jnp.float32),
             pltpu.VMEM((voxels, width), jnp.float32),
             pltpu.VMEM((voxels, width), jnp.float32),
-            dma((8, PIECES)), dma((8, PIECES)), dma((8,)), dma((8,)), dma((3,)), dma, dma((chunks,)), dma((chunks,)),
+            dma, dma((chunks,)), dma((chunks,)),
         ],
         compiler_params=pltpu.CompilerParams(
-            collective_id=0, has_side_effects=True, vmem_limit_bytes=40 * 1024 * 1024
+            collective_id=1 if paired else None, has_side_effects=paired, vmem_limit_bytes=24 * 1024 * 1024
         ),
         cost_estimate=pl.CostEstimate(
-            flops=2 * voxels * offsets * width * out_width, bytes_accessed=6 * 1024 * 1024, transcendentals=0
+            flops=2 * voxels * offsets * width * out_width, bytes_accessed=8 * 1024 * 1024, transcendentals=0
         ),
-    )(features, weights, send_rows, gather_map)
+    )(table.reshape(9 * voxels + 8, 1, width), idx, features, weights)
     if paired:
         return made
     return lax.psum_scatter(made, "chan", scatter_dimension=1, tiled=True).astype(jnp.bfloat16)

time: 98.7 us -> 102 us (1.033)
  Pallas kernels: 93.7 us -> 95.9 us
    pallas_call x1 -> x2, Pallas kernels: 93.7 us -> 95.9 us  [the longest x1 67 us: local(): pl.pallas_call(functools.partial(convolve, paired), out_shape=result, in_...]
    unnamed x9 -> x11, local copies, waits for them, and re-layouts: 4.77 us -> 5.72 us
where the time goes in v3:
time: 102 us
  Pallas kernels  95.9 us (94%)
  local copies, waits for them, and re-layouts  5.72 us (6%)
    pallas_call x1, Pallas kernels, local(): pl.pallas_call(functools.partial(convolve, paired), out_shape=result, in_...  67 us
    pallas_call x1, Pallas kernels, local(): pl.pallas_call(functools.partial(exchange, grid_rows), out_shape=(jax.Sha...  28.9 us
    unnamed x11, local copies, waits for them, and re-layouts  5.72 us

profile of v3, /device:TPU:2, one launch (start us, length us, event | category | flops | bytes accessed | tf_op | source)
XLA Modules:
  0.0 101.6 jit_solution(8286098454098875410)
XLA Ops:
  0.0 0.0 copy-start.1
  0.0 0.9 copy-done.1
  1.0 0.0 copy-start.3
  1.0 0.9 copy-done.3
  1.9 0.0 copy-start.4
  1.9 0.7 copy-done.4
  2.6 28.9 %shard_map.46 = (f32[9224,128]{1,0:T(8,128)S(1)}, s32[27,1024]{1,0:T(8,128)S(1)}) custom-call(bf16[1024,128]{1,0:T(8,128)(2,1)S(1)} %copy-done.1, s32[1,8,768]{2,1,0:T(8,128)S(1)} %copy-done.4, s32[27,1024]{1,0:T(8,128)S(1)} %copy-done.3), custom_call_target="tpu_custom_call" | custom-call | bytes 67108864 | tf_op jit(solution)/shard_map/pallas_call | solution.py:270
  31.5 0.0 copy-start
  31.5 1.5 %copy-done = bf16[27,128,256]{2,1,0:T(8,128)(2,1)S(1)} copy-done((bf16[27,128,256]{2,1,0:T(8,128)(2,1)S(1)}, bf16[27,128,256]{2,1,0:T(8,128)(2,1)}, u32[]{:S(2)}) %copy-start) | copy-done | bytes 1769496
  32.9 0.0 copy-start.2
  32.9 0.9 copy-done.2
  33.9 67.0 %shard_map.47 = bf16[1024,128]{1,0:T(8,128)(2,1)S(1)} custom-call(f32[9224,1,128]{2,1,0:T(1,128)S(1)} %bitcast.1, s32[27,1024]{1,0:T(8,128)S(1)} %get-tuple-element.8.idx, bf16[1024,128]{1,0:T(8,128)(2,1)S(1)} %copy-done.2, bf16[27,128,256]{2,1,0:T(8,128)(2,1)S(1)} %copy-done), custom_call_target="tpu_custom_call" | custom-call | flops 1811939328 | bytes 8388608 | tf_op jit(solution)/shard_map/pallas_call | solution.py:289
  100.9 0.7 copy.6
Async XLA Ops:
  0.0 0.9 copy-start.1
  1.0 0.9 copy-start.3
  1.9 0.7 copy-start.4
  31.5 1.5 %copy-start = (bf16[27,128,256]{2,1,0:T(8,128)(2,1)S(1)}, bf16[27,128,256]{2,1,0:T(8,128)(2,1)}, u32[]{:S(2)}) copy-start(bf16[27,128,256]{2,1,0:T(8,128)(2,1)} %weights.1) | copy-start | bytes 5308420
  32.9 0.9 copy-start.2

commit v4 on v3

--- a/solution.py
+++ b/solution.py
@@ -109,6 +109,9 @@
         lut[slot] = jnp.where(entry < voxels, entry + (1 + slot) * voxels, zero_row)
 
     own_tiles = voxels // LANES
+    chunk_tiles = CHUNK // LANES
+    for chunk in range(voxels // CHUNK):
+        idx[chunk, pl.ds(idx.shape[1] - 8, 8), :] = jnp.full((8, CHUNK), zero_row, jnp.int32)
 
     def compose(col, _):
         lanes = pl.ds(pl.multiple_of(col * LANES, LANES), LANES)
@@ -127,7 +130,7 @@
                     found = jnp.take_along_axis(line, within[i], axis=1, mode="promise_in_bounds")
                     result[i] = jnp.where(tiles[i] == number, found, result[i])
         for start, value in zip(starts, result):
-            idx[pl.ds(start, 8), lanes] = value
+            idx[col // chunk_tiles, pl.ds(start, 8), pl.ds(pl.multiple_of(col % chunk_tiles * LANES, LANES), LANES)] = value
         return 0
 
     lax.fori_loop(0, own_tiles, compose, 0)
@@ -191,11 +194,11 @@
     def offset_of(number):
         return number + (number >= centre).astype(jnp.int32)
 
-    def gather(buf, pair, base):
+    def gather(buf, pair, chunk):
         for half in range(2):
             offset = offset_of(2 * pair + half)
             for first in range(0, CHUNK, GROUP):
-                taken = [table[idx_s[offset, base + first + v]] for v in range(GROUP)]
+                taken = [table[idx_s[chunk, offset, first + v]] for v in range(GROUP)]
                 for v in range(GROUP):
                     buf[pl.ds(first + v, 1), pl.ds(half * LANES, LANES)] = taken[v]
 
@@ -218,16 +221,15 @@
         )
 
     def step(chunk, _):
-        base = chunk * CHUNK
-        span = pl.ds(pl.multiple_of(base, CHUNK), CHUNK)
+        span = pl.ds(pl.multiple_of(chunk * CHUNK, CHUNK), CHUNK)
         acc[...] = jnp.dot(feat[span, :], weights[centre], preferred_element_type=jnp.float32)
-        gather(buf_a, jnp.int32(0), base)
+        gather(buf_a, jnp.int32(0), chunk)
 
         def two(i, _):
             product(buf_a, 2 * i)
-            gather(buf_b, 2 * i + 1, base)
+            gather(buf_b, 2 * i + 1, chunk)
             product(buf_b, 2 * i + 1)
-            gather(buf_a, 2 * i + 2, base)
+            gather(buf_a, 2 * i + 2, chunk)
             return 0
 
         lax.fori_loop(0, (pairs - 1) // 2, two, 0)
@@ -264,6 +266,7 @@
         weights = jnp.pad(weights, ((0, 0), (0, LANES - own_width), (0, 0)))
     width = LANES
     chunks = voxels // CHUNK
+    maps = (chunks, pl.cdiv(offsets, 8) * 8, CHUNK)
     dma = pltpu.SemaphoreType.DMA
     result = jax.ShapeDtypeStruct((voxels, width) if paired else (voxels, out_width), jnp.bfloat16 if paired else jnp.float32)
     vmem = pl.BlockSpec(memory_space=pltpu.VMEM)
@@ -271,7 +274,7 @@
         functools.partial(exchange, grid_rows),
         out_shape=(
             jax.ShapeDtypeStruct((9 * voxels + 8, width), jnp.float32),
-            jax.ShapeDtypeStruct((offsets, voxels), jnp.int32),
+            jax.ShapeDtypeStruct(maps, jnp.int32),
         ),
         in_specs=[vmem] * 3,
         out_specs=(vmem, vmem),
@@ -292,7 +295,7 @@
         in_specs=[vmem] * 4,
         out_specs=vmem,
         scratch_shapes=[
-            pltpu.SMEM((offsets, voxels), jnp.int32),
+            pltpu.SMEM(maps, jnp.int32),
             pltpu.VMEM((CHUNK, 2 * width), jnp.float32),
             pltpu.VMEM((CHUNK, 2 * width), jnp.float32),
             pltpu.VMEM((CHUNK, out_width), jnp.float32),

time: 102 us -> 74.4 us (0.73)
  Pallas kernels: 95.9 us -> 68.4 us
    pallas_call x1, Pallas kernels: 67 us -> 39.5 us  [local(): pl.pallas_call(functools.partial(convolve, paired), out_shape=result, in_...]
where the time goes in v4:
time: 74.4 us; the launch traced here: 74.1 us
  Pallas kernels  68.4 us (92%)
  local copies, waits for them, and re-layouts  5.72 us (8%)
    pallas_call x1, Pallas kernels, local(): pl.pallas_call(functools.partial(convolve, paired), out_shape=result, in_...  39.5 us
    pallas_call x1, Pallas kernels, local(): pl.pallas_call(functools.partial(exchange, grid_rows), out_shape=(jax.Sha...  28.9 us
    unnamed x11, local copies, waits for them, and re-layouts  5.72 us

profile of v4, /device:TPU:2, one launch (start us, length us, event | category | flops | bytes accessed | tf_op | source)
XLA Modules:
  0.0 74.1 jit_solution(3771516734754523373)
XLA Ops:
  0.0 0.0 copy-start.1
  0.0 0.9 %copy-done.1 = bf16[1024,128]{1,0:T(8,128)(2,1)S(1)} copy-done((bf16[1024,128]{1,0:T(8,128)(2,1)S(1)}, bf16[1024,128]{1,0:T(8,128)(2,1)}, u32[]{:S(2)}) %copy-start.1) | copy-done | bytes 262168
  1.0 0.0 copy-start.3
  1.0 0.9 %copy-done.3 = s32[27,1024]{1,0:T(8,128)S(1)} copy-done((s32[27,1024]{1,0:T(8,128)S(1)}, s32[27,1024]{1,0:T(8,128)}, u32[]{:S(2)}) %copy-start.3) | copy-done | bytes 110616
  1.9 0.0 copy-start.4
  1.9 0.7 copy-done.4
  2.6 28.9 %shard_map.46 = (f32[9224,128]{1,0:T(8,128)S(1)}, s32[4,32,256]{2,1,0:T(8,128)S(1)}) custom-call(bf16[1024,128]{1,0:T(8,128)(2,1)S(1)} %copy-done.1, s32[1,8,768]{2,1,0:T(8,128)S(1)} %copy-done.4, s32[27,1024]{1,0:T(8,128)S(1)} %copy-done.3), custom_call_target="tpu_custom_call" | custom-call | bytes 67108864 | tf_op jit(solution)/shard_map/pallas_call | solution.py:273
  31.5 0.0 copy-start
  31.5 1.5 %copy-done = bf16[27,128,256]{2,1,0:T(8,128)(2,1)S(1)} copy-done((bf16[27,128,256]{2,1,0:T(8,128)(2,1)S(1)}, bf16[27,128,256]{2,1,0:T(8,128)(2,1)}, u32[]{:S(2)}) %copy-start) | copy-done | bytes 1769496
  32.9 0.0 copy-start.2
  32.9 0.9 %copy-done.2 = bf16[1024,128]{1,0:T(8,128)(2,1)S(1)} copy-done((bf16[1024,128]{1,0:T(8,128)(2,1)S(1)}, bf16[1024,128]{1,0:T(8,128)(2,1)}, u32[]{:S(2)}) %copy-start.2) | copy-done | bytes 262168
  33.9 39.5 %shard_map.47 = bf16[1024,128]{1,0:T(8,128)(2,1)S(1)} custom-call(f32[9224,1,128]{2,1,0:T(1,128)S(1)} %bitcast.1, s32[4,32,256]{2,1,0:T(8,128)S(1)} %get-tuple-element.8.idx, bf16[1024,128]{1,0:T(8,128)(2,1)S(1)} %copy-done.2, bf16[27,128,256]{2,1,0:T(8,128)(2,1)S(1)} %copy-done), custom_call_target="tpu_custom_call" | custom-call | flops 1811939328 | bytes 8388608 | tf_op jit(solution)/shard_map/pallas_call | solution.py:292
  73.4 0.7 copy.6
Async XLA Ops:
  0.0 0.9 %copy-start.1 = (bf16[1024,128]{1,0:T(8,128)(2,1)S(1)}, bf16[1024,128]{1,0:T(8,128)(2,1)}, u32[]{:S(2)}) copy-start(bf16[1024,128]{1,0:T(8,128)(2,1)} %feat.3) | copy-start | bytes 786436
  1.0 0.9 %copy-start.3 = (s32[27,1024]{1,0:T(8,128)S(1)}, s32[27,1024]{1,0:T(8,128)}, u32[]{:S(2)}) copy-start(s32[27,1024]{1,0:T(8,128)} %gmap.1) | copy-start | bytes 331780
  1.9 0.7 copy-start.4
  31.5 1.5 %copy-start = (bf16[27,128,256]{2,1,0:T(8,128)(2,1)S(1)}, bf16[27,128,256]{2,1,0:T(8,128)(2,1)}, u32[]{:S(2)}) copy-start(bf16[27,128,256]{2,1,0:T(8,128)(2,1)} %weights.1) | copy-start | bytes 5308420
  32.9 0.9 %copy-start.2 = (bf16[1024,128]{1,0:T(8,128)(2,1)S(1)}, bf16[1024,128]{1,0:T(8,128)(2,1)}, u32[]{:S(2)}) copy-start(bf16[1024,128]{1,0:T(8,128)(2,1)} %feat.3) | copy-start | bytes 786436

commit v5 on v2

--- a/solution.py
+++ b/solution.py
@@ -121,6 +121,9 @@
         lut[slot] = jnp.where(entry < voxels, entry + (1 + slot) * voxels, zero_row)
 
     own_tiles = voxels // LANES
+    chunk_tiles = CHUNK // LANES
+    for chunk in range(voxels // CHUNK):
+        idx[chunk, pl.ds(idx.shape[1] - 8, 8), :] = jnp.full((8, CHUNK), zero_row, jnp.int32)
 
     def compose(col, _):
         lanes = pl.ds(pl.multiple_of(col * LANES, LANES), LANES)
@@ -139,7 +142,7 @@
                     found = jnp.take_along_axis(line, within[i], axis=1, mode="promise_in_bounds")
                     result[i] = jnp.where(tiles[i] == number, found, result[i])
         for start, value in zip(starts, result):
-            idx[pl.ds(start, 8), lanes] = value
+            idx[col // chunk_tiles, pl.ds(start, 8), pl.ds(pl.multiple_of(col % chunk_tiles * LANES, LANES), LANES)] = value
         return 0
 
     lax.fori_loop(0, own_tiles, compose, 0)
@@ -178,11 +181,11 @@
     def offset_of(number):
         return number + (number >= centre).astype(jnp.int32)
 
-    def gather(buf, pair, base):
+    def gather(buf, pair, chunk):
         for half in range(2):
             offset = offset_of(2 * pair + half)
             for first in range(0, CHUNK, GROUP):
-                taken = [table[pl.ds(idx_s[offset, base + first + v], 1), :] for v in range(GROUP)]
+                taken = [table[pl.ds(idx_s[chunk, offset, first + v], 1), :] for v in range(GROUP)]
                 for v in range(GROUP):
                     buf[pl.ds(first + v, 1), pl.ds(half * LANES, LANES)] = taken[v]
 
@@ -208,13 +211,13 @@
         base = chunk * CHUNK
         span = pl.ds(pl.multiple_of(base, CHUNK), CHUNK)
         acc[...] = jnp.dot(feat[span, :], weights[centre], preferred_element_type=jnp.float32)
-        gather(buf_a, jnp.int32(0), base)
+        gather(buf_a, jnp.int32(0), chunk)
 
         def two(i, _):
             product(buf_a, 2 * i)
-            gather(buf_b, 2 * i + 1, base)
+            gather(buf_b, 2 * i + 1, chunk)
             product(buf_b, 2 * i + 1)
-            gather(buf_a, 2 * i + 2, base)
+            gather(buf_a, 2 * i + 2, chunk)
             return 0
 
         lax.fori_loop(0, (pairs - 1) // 2, two, 0)
@@ -267,6 +270,7 @@
         weights = jnp.pad(weights, ((0, 0), (0, LANES - own_width), (0, 0)))
     width = LANES
     chunks = voxels // CHUNK
+    maps = (chunks, pl.cdiv(offsets, 8) * 8, CHUNK)
     dma = pltpu.SemaphoreType.DMA
     result = jax.ShapeDtypeStruct((voxels, width) if paired else (voxels, out_width), jnp.bfloat16 if paired else jnp.float32)
     made = pl.pallas_call(
@@ -282,8 +286,8 @@
             pltpu.VMEM((8, 1, slots), jnp.int32),
             pltpu.VMEM((8, 1, slots), jnp.int32),
             pltpu.VMEM((9 * voxels + 8, width), jnp.float32),
-            pltpu.VMEM((offsets, voxels), jnp.int32),
-            pltpu.SMEM((offsets, voxels), jnp.int32),
+            pltpu.VMEM(maps, jnp.int32),
+            pltpu.SMEM(maps, jnp.int32),
             pltpu.VMEM((CHUNK, 2 * width), jnp.float32),
             pltpu.VMEM((CHUNK, 2 * width), jnp.float32),
             pltpu.VMEM((CHUNK, out_width), jnp.float32),
@@ -293,7 +297,7 @@
             dma((8, PIECES)), dma((8, PIECES)), dma((8,)), dma((8,)), dma((3,)), dma, dma((chunks,)), dma((chunks,)),
         ],
         compiler_params=pltpu.CompilerParams(
-            collective_id=0, has_side_effects=True, vmem_limit_bytes=40 * 1024 * 1024
+            collective_id=0, has_side_effects=True, vmem_limit_bytes=64 * 1024 * 1024
         ),
         cost_estimate=pl.CostEstimate(
             flops=2 * voxels * offsets * width * out_width, bytes_accessed=6 * 1024 * 1024, transcendentals=0

time: 98.7 us -> 68.8 us (0.70)
  Pallas kernels: 93.7 us -> 67 us
  local copies, waits for them, and re-layouts: 4.77 us -> 1.67 us
    pallas_call x1, Pallas kernels: 93.7 us -> 67 us  [local(): pl.pallas_call(functools.partial(kernel, grid_rows, paired), out_shape=re...]
    unnamed x9 -> x1, local copies, waits for them, and re-layouts: 4.77 us -> 1.67 us
where the time goes in v5:
time: 68.8 us; the launch traced here: 68.7 us
  Pallas kernels  67 us (97%)
  local copies, waits for them, and re-layouts  1.67 us (2%)
    pallas_call x1, Pallas kernels, local(): pl.pallas_call(functools.partial(kernel, grid_rows, paired), out_shape=re...  67 us
    unnamed x1, local copies, waits for them, and re-layouts  1.67 us

profile of v5, /device:TPU:2, one launch (start us, length us, event | category | flops | bytes accessed | tf_op | source)
XLA Modules:
  0.0 68.7 jit_solution(10522927862226970292)
XLA Ops:
  0.0 67.0 %shard_map.46 = bf16[1024,128]{1,0:T(8,128)(2,1)} custom-call(bf16[1024,128]{1,0:T(8,128)(2,1)} %feat_hbm.1, bf16[27,128,256]{2,1,0:T(8,128)(2,1)} %weights_hbm.1, s32[1,8,768]{2,1,0:T(8,128)} %send_rows.1, s32[27,1024]{1,0:T(8,128)} %gmap_hbm.1), custom_call_target="tpu_custom_call" | custom-call | flops 1811939328 | bytes 6291456 | tf_op jit(solution)/shard_map/pallas_call | solution.py:276
  67.0 1.7 %copy.6 = bf16[1024,128]{1,0:T(8,128)(2,1)} copy(bf16[1024,128]{1,0:T(8,128)(2,1)} %shard_map.46) | data formatting | bytes 524288
